TPU v7x, 256 devices: a whole 4x4x8 slice. The times are simulated.
256 devices in a mesh: wa: 8 (over z), vert: 32 (over y, x, core).
Axes of the slice: x: 4, y: 4, z: 8, core: 2. Of those that a mesh axis runs over, the one named last changes fastest.
Arguments:
- hidden_in: bfloat16 [384, 8192], P(None, 'wa')
- gate_levels: bfloat16 [8192, 28672], P('wa', 'vert'), may hold values from -127 to 127, as said below
- up_levels: bfloat16 [8192, 28672], P('wa', 'vert'), may hold values from -127 to 127, as said below
- gate_scale: float32 [28672], P('vert'), as said below
- up_scale: float32 [28672], P('vert'), as said below
- down_levels: bfloat16 [28672, 8192], P('vert', 'wa'), may hold values from -127 to 127, as said below
- down_scale: float32 [8192], P('wa'), as said below
- norm_gain: float32 [8192], P('wa'), may hold values from 0.5 to 1.5
- head_weight: bfloat16 [8192, 16000], P('wa', 'vert')
- reward_states: bfloat16 [8, 384, 4096], P('wa', None, 'vert'), may hold values from -6 to 6
- reward_gain: float32 [8, 4096], P('wa'), may hold values from 0.5 to 1.5
- reward_heads: bfloat16 [8, 4096, 16000], P('wa', None, 'vert')
- preference: int32 [384, 8], P(None, 'wa'), may hold values from 0 to 16
- token_ids: int32 [384], P('wa'), may hold values from 0 to 15999
Outputs:
- log_probs: float32 [384, 16000], P('wa', 'vert')
- chosen: float32 [384], P('wa')
Inputs may be any that keep to these rules, and one draw needn't show every extreme that they name: `gate_levels`: whole numbers. `up_levels`: whole numbers. `down_levels`: whole numbers. `gate_scale`: positive. `up_scale`: positive. `down_scale`: positive.
All inputs are finite; a program needn't handle non-finite values.
Results may differ from a plain program's by a relative error of at most 0.0025.
Values may be sent and summed in bfloat16 or wider, within the bound.
No kernel may reach another device: no remote copies, remote signals or barrier semaphores. Data moves between devices by JAX's collectives and lax.ppermute only.
A program may use at most 64 MiB of HBM per device.

v0:
```python
import jax
import jax.numpy as jnp
from jax import lax
from jax.sharding import PartitionSpec as P

D = 8192


def log_total(values):
    local_top = jnp.max(values, axis=-1)
    top = lax.pmax(local_top, "vert")
    total = lax.psum(jnp.sum(jnp.exp(values - top[..., None]), axis=-1), "vert")
    return top + jnp.log(total)


def normalize(resid, norm_gain):
    squares = lax.psum(jnp.sum(resid * resid, axis=1), "wa")
    return (resid * lax.rsqrt(squares[:, None] / D + 1e-05) * norm_gain).astype(jnp.bfloat16)


def local(
    hidden_in,
    gate_levels,
    up_levels,
    gate_scale,
    up_scale,
    down_levels,
    down_scale,
    norm_gain,
    head_weight,
    reward_states,
    reward_gain,
    reward_heads,
    preference,
    token_ids,
):
    gate_part = jnp.dot(hidden_in, gate_levels, preferred_element_type=jnp.float32)
    up_part = jnp.dot(hidden_in, up_levels, preferred_element_type=jnp.float32)
    gate, up = lax.psum((gate_part, up_part), "wa")
    hidden = (jax.nn.silu(gate * gate_scale) * (up * up_scale)).astype(jnp.bfloat16)
    down_part = jnp.dot(hidden, down_levels, preferred_element_type=jnp.float32)
    down = lax.psum(down_part, "vert") * down_scale
    resid = hidden_in.astype(jnp.float32) + down
    normed = normalize(resid, norm_gain)
    base_part = jnp.dot(normed, head_weight, preferred_element_type=jnp.float32)
    states = lax.all_gather(reward_states, "vert", axis=2, tiled=True)
    state_values = states.astype(jnp.float32)
    state_scale = lax.rsqrt(jnp.mean(state_values * state_values, axis=2, keepdims=True) + 1e-05)
    reward_normed = (state_values * state_scale * reward_gain[:, None, :]).astype(jnp.bfloat16)
    reward_logits = jnp.einsum(
        "rnd,rdv->rnv", reward_normed, reward_heads, preferred_element_type=jnp.float32
    )
    reward_logp = reward_logits - log_total(reward_logits)[..., None]
    weights = preference.astype(jnp.float32).T / 16.0
    weighted = jnp.sum(weights[:, :, None] * reward_logp, axis=0)
    base_rows, reward_rows = (
        lax.psum_scatter(base_part, "wa", scatter_dimension=0, tiled=True),
        lax.psum_scatter(weighted, "wa", scatter_dimension=0, tiled=True),
    )
    base_logp = base_rows - log_total(base_rows)[:, None]
    mix = base_logp + reward_rows
    log_probs = mix - log_total(mix)[:, None]
    columns = log_probs.shape[1]
    vocab_index = lax.axis_index("vert") * columns + lax.iota(jnp.int32, columns)
    picked = jnp.sum(jnp.where(vocab_index[None, :] == token_ids[:, None], log_probs, 0.0), axis=1)
    chosen = lax.psum(picked, "vert")
    return (log_probs, chosen)


def solution(mesh):
    return jax.shard_map(
        local,
        mesh=mesh,
        in_specs=(
            P(None, "wa"),
            P("wa", "vert"),
            P("wa", "vert"),
            P("vert"),
            P("vert"),
            P("vert", "wa"),
            P("wa"),
            P("wa"),
            P("wa", "vert"),
            P("wa", None, "vert"),
            P("wa", None),
            P("wa", None, "vert"),
            P(None, "wa"),
            P("wa"),
        ),
        out_specs=(P("wa", "vert"), P("wa")),
        check_vma=False,
    )
```

profile of v0, /device:TPU:1, one launch (start us, length us, event | category | flops | bytes accessed | tf_op | source)
XLA Modules:
  0.0 702.5 jit_solution(15787238454085852242)
XLA Ops:
  7.2 3.9 fusion.17
  11.2 2.0 fusion.18
  13.3 89.1 %all-reduce.8.cloned.1.call-done = (f32[384,896]{1,0:T(8,128)}, f32[384,896]{1,0:T(8,128)}) async-done(((f32[384,896]{1,0:T(8,128)}, f32[384,896]{1,0:T(8,128)}), (f32[384,896]{1,0:T(8,128)}, f32[384,896]{1,0:T(8,128)})) %all-reduce.8.cloned.1.call-update) | async-done | bytes 2752528 | tf_op jit(solution)/shard_map/psum | solution.py:39
  102.5 3.9 fusion.13
  106.5 0.0 reduce-scatter.7.cloned.1.call-start
  106.5 116.9 %all-reduce.6.cloned.1.call-done = f32[384,1024]{1,0:T(8,128)} async-done(((f32[384,1024]{1,0:T(8,128)}), f32[384,1024]{1,0:T(8,128)}) %all-reduce.6.cloned.1.call-update) | async-done | bytes 1572880 | tf_op jit(solution)/shard_map/psum | solution.py:42
  223.4 2.1 multiply_reduce_fusion
  225.4 13.7 %psum.59 = f32[384]{0:T(512)S(1)} all-reduce(f32[384]{0:T(512)S(1)} %multiply_reduce_fusion), channel_id=1, replica_groups=mesh['wa'=8,'vert'=32] {'wa'}, use_global_device_ids=true, to_apply=%region_4.5 | all-reduce | flops 384 | bytes 3072 | tf_op jit(solution)/shard_map/psum | solution.py:17
  239.1 3.0 fusion.9
  242.2 0.5 all-gather.2.cloned.1.call-update
  242.8 33.5 %reduce-scatter.7.cloned.1.call-done = f32[48,500]{1,0:T(8,128)} async-done(((f32[384,500]{1,0:T(8,128)}), f32[48,500]{1,0:T(8,128)}) %reduce-scatter.7.cloned.1.call-update) | async-done | bytes 96016
  276.3 1.0 copy.23
  277.4 1.1 reduce_max.29
  278.5 55.9 %all-gather.2.cloned.1.call-done = bf16[1,384,4096]{2,1,0:T(8,128)(2,1)} async-done(((bf16[1,384,128]{2,1,0:T(8,128)(2,1)}), bf16[1,384,4096]{2,1,0:T(8,128)(2,1)}) %all-gather.2.cloned.1.call-update) | async-done | bytes 3145744 | tf_op jit(solution)/shard_map/all_gather | solution.py:46
  334.3 2.7 fusion
  337.1 0.1 copy-done.2
  337.2 4.6 fusion.16
  341.8 62.3 %all-reduce.1 = (f32[1,384]{1,0:T(1,128)S(1)}, f32[48]{0:T(128)S(1)}) all-reduce(f32[1,384]{1,0:T(1,128)S(1)} %reduce_max.31, f32[48]{0:T(128)S(1)} %reduce_max.29), channel_id=1, replica_groups=mesh['wa'=8,'vert'=32] {'vert'}, use_global_device_ids=true, to_apply=%region_12.13 | all-reduce | flops 432 | bytes 3456 | tf_op jit(solution)/shard_map/pmax | solution.py:11
  404.1 0.2 exponential_reduce_fusion
  404.3 0.1 exponential_reduce_fusion.2
  404.4 65.2 %all-reduce = (f32[1,384]{1,0:T(1,128)S(1)}, f32[48]{0:T(128)S(1)}) all-reduce(f32[1,384]{1,0:T(1,128)S(1)} %reduce_sum.64, f32[48]{0:T(128)S(1)} %exponential_reduce_fusion.2), channel_id=1, replica_groups=mesh['wa'=8,'vert'=32] {'vert'}, use_global_device_ids=true, to_apply=%region_14.15 | all-reduce | flops 432 | bytes 3456 | tf_op jit(solution)/shard_map/psum | solution.py:12
  469.6 0.1 subtract_multiply_fusion
  469.7 1.2 copy.24
  471.0 29.6 %reduce-scatter.9.cloned.1.call-done = f32[48,500]{1,0:T(8,128)} async-done(((f32[384,500]{1,0:T(8,128)}), f32[48,500]{1,0:T(8,128)}) %reduce-scatter.9.cloned.1.call-update) | async-done | bytes 96016
  500.5 1.0 copy.25
  501.6 0.1 fusion.15
  501.7 67.5 %pmax.23 = f32[48]{0:T(128)S(1)} all-reduce(f32[48]{0:T(128)S(1)} %get-tuple-element.14), channel_id=1, replica_groups=mesh['wa'=8,'vert'=32] {'vert'}, use_global_device_ids=true, to_apply=%region_17.18 | all-reduce | flops 48 | bytes 384 | tf_op jit(solution)/shard_map/pmax | solution.py:11
  569.2 0.1 exponential_reduce_fusion.1
  569.3 62.7 %psum.62 = f32[48]{0:T(128)S(1)} all-reduce(f32[48]{0:T(128)S(1)} %exponential_reduce_fusion.1), channel_id=1, replica_groups=mesh['wa'=8,'vert'=32] {'vert'}, use_global_device_ids=true, to_apply=%region_19.20 | all-reduce | flops 48 | bytes 384 | tf_op jit(solution)/shard_map/psum | solution.py:12
  632.0 0.2 select_reduce_fusion
  632.1 0.8 copy.20
  632.9 63.2 %psum.63 = f32[48]{0:T(128)} all-reduce(f32[48]{0:T(128)S(1)} %get-tuple-element.12), channel_id=1, replica_groups=mesh['wa'=8,'vert'=32] {'vert'}, use_global_device_ids=true, to_apply=%region_21.22 | all-reduce | flops 48 | bytes 384 | tf_op jit(solution)/shard_map/psum | solution.py:66
  (45 shorter events, 0.4 us)
Async XLA Ops:
  7.2 95.3 %copy-start = (bf16[896,1024]{1,0:T(8,128)(2,1)S(1)}, bf16[896,1024]{1,0:T(8,128)(2,1)}, u32[]{:S(2)}) copy-start(bf16[896,1024]{1,0:T(8,128)(2,1)} %param.19) | copy-start | bytes 5505028
  7.2 4.0 copy-start.3
  7.2 95.3 %all-reduce.8.cloned.1.call-start = ((), (), s32[]{:S(2)}) async-start(), calls=%async_computation.6 | async-start | bytes 5505024 | tf_op jit(solution)/shard_map/psum | solution.py:39
  7.2 4.0 copy-start.10
  13.2 89.2 %copy-start.12 = (f32[896]{0:T(1024)S(1)}, f32[896]{0:T(1024)}, u32[]{:S(2)}) copy-start(f32[896]{0:T(1024)} %param.18) | copy-start | bytes 10756
  13.2 89.2 %copy-start.13 = (f32[896]{0:T(1024)S(1)}, f32[896]{0:T(1024)}, u32[]{:S(2)}) copy-start(f32[896]{0:T(1024)} %param.17) | copy-start | bytes 10756
  13.3 210.1 %all-reduce.6.cloned.1.call-start = ((), (), s32[]{:S(2)}) async-start(), calls=%async_computation.2 | async-start | bytes 3145728 | tf_op jit(solution)/shard_map/psum | solution.py:42
  106.4 116.9 %copy-start.6 = (f32[1024]{0:T(1024)S(1)}, f32[1024]{0:T(1024)}, u32[]{:S(2)}) copy-start(f32[1024]{0:T(1024)} %param.20) | copy-start | bytes 12292
  106.4 132.7 %copy-start.7 = (f32[1024]{0:T(1024)S(1)}, f32[1024]{0:T(1024)}, u32[]{:S(2)}) copy-start(f32[1024]{0:T(1024)} %param.21) | copy-start | bytes 12292
  106.5 169.9 %reduce-scatter.7.cloned.1.call-start = ((), (), s32[]{:S(2)}) async-start(), calls=%async_computation.4 | async-start | bytes 884736
  223.4 15.8 %copy-start.1 = (f32[384,1024]{1,0:T(8,128)S(1)}, f32[384,1024]{1,0:T(8,128)}, u32[]{:S(2)}) copy-start(f32[384,1024]{1,0:T(8,128)} %all-reduce.6.cloned.1.call-done) | copy-start | bytes 4718596
  239.1 3.6 copy-start.8
  242.1 92.2 %all-gather.2.cloned.1.call-start = ((), (), s32[]{:S(2)}) async-start(), calls=%async_computation.3 | async-start | bytes 3244032 | tf_op jit(solution)/shard_map/all_gather | solution.py:46
  242.7 257.8 %reduce-scatter.9.cloned.1.call-start = ((), (), s32[]{:S(2)}) async-start(), calls=%async_computation.5 | async-start | bytes 884736
  277.3 126.9 %copy-start.4 = (f32[48,500]{0,1:T(8,128)}, f32[48,500]{0,1:T(8,128)S(1)}, u32[]{:S(2)}) copy-start(f32[48,500]{0,1:T(8,128)S(1)} %copy.23) | copy-start | bytes 288004
  277.4 59.7 %copy-start.11 = (f32[1,4096]{1,0:T(1,128)S(1)}, f32[1,4096]{1,0:T(1,128)}, u32[]{:S(2)}) copy-start(f32[1,4096]{1,0:T(1,128)} %param.24) | copy-start | bytes 49156
  334.3 2.8 copy-start.2
  469.7 31.8 %copy-start.5 = (f32[48,500]{0,1:T(8,128)S(1)}, f32[48,500]{0,1:T(8,128)}, u32[]{:S(2)}) copy-start(f32[48,500]{0,1:T(8,128)} %copy-done.4) | copy-start | bytes 288004
  469.7 162.2 %copy-start.9 = (s32[48]{0:T(128)S(1)}, s32[48]{0:T(128)}, u32[]{:S(2)}) copy-start(s32[48]{0:T(128)} %param.27) | copy-start | bytes 580
Sparse Core Ops, SparseCore 0:
  13.4 89.0 all-reduce.7
  106.6 116.7 all-reduce.5
  242.3 34.0 reduce-scatter.6
  279.0 55.3 all-gather.1
  471.1 29.4 reduce-scatter.8
where the time goes:
time: 703 us
  blocking collectives  335 us (48%)
  waiting for transfers between devices  326 us (46%)
  matrix products  17.5 us (2%)
  between operations  13.9 us (2%)
    pmax x2, blocking collectives, log_total(): top = lax.pmax(local_top, 'vert')  130 us
    psum x2, blocking collectives, log_total(): total = lax.psum(jnp.sum(jnp.exp(values - top[..., None]), axis=-1), 'vert')  128 us
    psum x1, waiting for transfers between devices, local(): down = lax.psum(down_part, 'vert') * down_scale  117 us
    psum x1, waiting for transfers between devices, local(): gate, up = lax.psum((gate_part, up_part), 'wa')  89.1 us
    unnamed x7, waiting for transfers between devices  63.7 us
    psum x1, blocking collectives, local(): chosen = lax.psum(picked, 'vert')  63.2 us
    all_gather x1, waiting for transfers between devices, local(): states = lax.all_gather(reward_states, 'vert', axis=2, tiled=True)  55.9 us
  transfers between devices with their start and end apart: 5, of which 5 were waited for; matrix products, arithmetic and copies ran while one was open for 0% of the time, Pallas kernels for 0%

commit v1 on v0

--- a/solution.py
+++ b/solution.py
@@ -43,7 +43,8 @@
     resid = hidden_in.astype(jnp.float32) + down
     normed = normalize(resid, norm_gain)
     base_part = jnp.dot(normed, head_weight, preferred_element_type=jnp.float32)
-    states = lax.all_gather(reward_states, "vert", axis=2, tiled=True)
+    sent = jnp.stack([reward_states] * lax.axis_size("vert"))
+    states = jnp.concatenate(lax.all_to_all(sent, "vert", 0, 0), axis=2)
     state_values = states.astype(jnp.float32)
     state_scale = lax.rsqrt(jnp.mean(state_values * state_values, axis=2, keepdims=True) + 1e-05)
     reward_normed = (state_values * state_scale * reward_gain[:, None, :]).astype(jnp.bfloat16)

time: 703 us -> 639 us (0.909)
  waiting for transfers between devices: 326 us -> 247 us
  starting transfers between devices: 0.2 us -> 8.93 us
    all_gather x1 -> x0, waiting for transfers between devices: 55.9 us -> none  [local(): states = lax.all_gather(reward_states, 'vert', axis=2, tiled=True)]
    psum x1, waiting for transfers between devices: 89.1 us -> 77.2 us  [local(): gate, up = lax.psum((gate_part, up_part), 'wa')]
    unnamed x7 -> x6, waiting for transfers between devices: 63.7 us -> 52.4 us
    all_to_all x0 -> x1, starting transfers between devices: none -> 8.77 us  [local(): states = jnp.concatenate(lax.all_to_all(sent, 'vert', 0, 0), axis=2)]
  transfers between devices with their start and end apart: 5 -> 5, of which waited for: 5 -> 4; matrix products, arithmetic and copies ran while one was open for 0% -> 3% of each run, Pallas kernels for 0% -> 0%
where the time goes in v1:
time: 639 us
  blocking collectives  337 us (53%)
  waiting for transfers between devices  247 us (39%)
  matrix products  15.3 us (2%)
  between operations  14 us (2%)
  other arithmetic  8.99 us (1%)
  starting transfers between devices  8.93 us (1%)
  local copies, waits for them, and re-layouts  7.82 us (1%)
    pmax x2, blocking collectives, log_total(): top = lax.pmax(local_top, 'vert')  135 us
    psum x2, blocking collectives, log_total(): total = lax.psum(jnp.sum(jnp.exp(values - top[..., None]), axis=-1), 'vert')  125 us
    psum x1, waiting for transfers between devices, local(): down = lax.psum(down_part, 'vert') * down_scale  117 us
    psum x1, waiting for transfers between devices, local(): gate, up = lax.psum((gate_part, up_part), 'wa')  77.2 us
    psum x1, blocking collectives, local(): chosen = lax.psum(picked, 'vert')  63.2 us
    unnamed x6, waiting for transfers between devices  52.4 us
    psum x1, blocking collectives, normalize(): squares = lax.psum(jnp.sum(resid * resid, axis=1), 'wa')  13.7 us
  transfers between devices with their start and end apart: 5, of which 4 were waited for; matrix products, arithmetic and copies ran while one was open for 3% of the time, Pallas kernels for 0%

profile of v1, /device:TPU:1, one launch (start us, length us, event | category | flops | bytes accessed | tf_op | source)
XLA Modules:
  0.0 638.8 jit_solution(884959455518435105)
XLA Ops:
  7.2 4.0 fusion.14
  11.2 2.1 fusion.13
  13.3 0.9 copy-done.5
  14.2 0.1 copy.27
  14.3 2.2 stack.2
  16.5 8.8 %all-to-all-start = ((bf16[32,1,384,128]{2,3,1,0:T(8,128)(2,1)}), bf16[32,1,384,128]{2,3,1,0:T(8,128)(2,1)}, u32[]{:S(2)}, u32[]{:S(2)}) async-start(bf16[32,1,384,128]{2,3,1,0:T(8,128)(2,1)} %stack.2), calls=%async_computation | async-start | bytes 6291456 | tf_op jit(solution)/shard_map/all_to_all | solution.py:47
  25.3 77.2 %all-reduce.8.cloned.1.call-done = (f32[384,896]{1,0:T(8,128)}, f32[384,896]{1,0:T(8,128)}) async-done(((f32[384,896]{1,0:T(8,128)}, f32[384,896]{1,0:T(8,128)}), (f32[384,896]{1,0:T(8,128)}, f32[384,896]{1,0:T(8,128)})) %all-reduce.8.cloned.1.call-update) | async-done | bytes 2752528 | tf_op jit(solution)/shard_map/psum | solution.py:39
  102.6 3.9 fusion.9
  106.6 116.9 %all-reduce.6.cloned.1.call-done = f32[384,1024]{1,0:T(8,128)} async-done(((f32[384,1024]{1,0:T(8,128)}), f32[384,1024]{1,0:T(8,128)}) %all-reduce.6.cloned.1.call-update) | async-done | bytes 1572880 | tf_op jit(solution)/shard_map/psum | solution.py:42
  223.5 2.1 multiply_reduce_fusion
  225.5 13.7 %psum.59 = f32[384]{0:T(512)S(1)} all-reduce(f32[384]{0:T(512)S(1)} %multiply_reduce_fusion), channel_id=1, replica_groups=mesh['wa'=8,'vert'=32] {'wa'}, use_global_device_ids=true, to_apply=%region_4.5 | all-reduce | flops 384 | bytes 3072 | tf_op jit(solution)/shard_map/psum | solution.py:17
  239.3 3.0 fusion.5
  242.4 2.7 fusion
  245.1 2.5 fusion.2
  247.6 0.6 copy-done.11
  248.2 2.3 fusion.12
  250.5 25.4 %reduce-scatter.7.cloned.1.call-done = f32[48,500]{1,0:T(8,128)} async-done(((f32[384,500]{1,0:T(8,128)}), f32[48,500]{1,0:T(8,128)}) %reduce-scatter.7.cloned.1.call-update) | async-done | bytes 96016
  275.9 1.0 reduce_max.29
  276.9 67.6 %all-reduce.1 = (f32[1,384]{1,0:T(1,128)S(1)}, f32[48]{0:T(128)S(1)}) all-reduce(f32[1,384]{1,0:T(1,128)S(1)} %reduce_max.31, f32[48]{0:T(128)S(1)} %reduce_max.29), channel_id=1, replica_groups=mesh['wa'=8,'vert'=32] {'vert'}, use_global_device_ids=true, to_apply=%region_12.13 | all-reduce | flops 432 | bytes 3456 | tf_op jit(solution)/shard_map/pmax | solution.py:11
  344.5 0.2 exponential_reduce_fusion
  344.7 1.0 copy.32
  345.8 62.7 %all-reduce = (f32[1,384]{1,0:T(1,128)S(1)}, f32[48]{0:T(128)S(1)}) all-reduce(f32[1,384]{1,0:T(1,128)S(1)} %reduce_sum.64, f32[48]{0:T(128)S(1)} %exponential_reduce_fusion.2), channel_id=1, replica_groups=mesh['wa'=8,'vert'=32] {'vert'}, use_global_device_ids=true, to_apply=%region_14.15 | all-reduce | flops 432 | bytes 3456 | tf_op jit(solution)/shard_map/psum | solution.py:12
  408.6 1.2 copy.33
  409.9 26.9 %reduce-scatter.9.cloned.1.call-done = f32[48,500]{1,0:T(8,128)} async-done(((f32[384,500]{1,0:T(8,128)}), f32[48,500]{1,0:T(8,128)}) %reduce-scatter.9.cloned.1.call-update) | async-done | bytes 96016
  436.8 1.0 copy.34
  437.8 0.1 fusion.11
  437.9 67.5 %pmax.23 = f32[48]{0:T(128)S(1)} all-reduce(f32[48]{0:T(128)S(1)} %get-tuple-element.14), channel_id=1, replica_groups=mesh['wa'=8,'vert'=32] {'vert'}, use_global_device_ids=true, to_apply=%region_17.18 | all-reduce | flops 48 | bytes 384 | tf_op jit(solution)/shard_map/pmax | solution.py:11
  505.4 0.1 exponential_reduce_fusion.1
  505.5 62.7 %psum.62 = f32[48]{0:T(128)S(1)} all-reduce(f32[48]{0:T(128)S(1)} %exponential_reduce_fusion.1), channel_id=1, replica_groups=mesh['wa'=8,'vert'=32] {'vert'}, use_global_device_ids=true, to_apply=%region_19.20 | all-reduce | flops 48 | bytes 384 | tf_op jit(solution)/shard_map/psum | solution.py:12
  568.2 0.2 select_reduce_fusion
  568.3 0.8 copy.29
  569.1 63.2 %psum.63 = f32[48]{0:T(128)} all-reduce(f32[48]{0:T(128)S(1)} %get-tuple-element.12), channel_id=1, replica_groups=mesh['wa'=8,'vert'=32] {'vert'}, use_global_device_ids=true, to_apply=%region_21.22 | all-reduce | flops 48 | bytes 384 | tf_op jit(solution)/shard_map/psum | solution.py:67
  (49 shorter events, 0.6 us)
Async XLA Ops:
  7.2 95.4 %copy-start = (bf16[896,1024]{1,0:T(8,128)(2,1)S(1)}, bf16[896,1024]{1,0:T(8,128)(2,1)}, u32[]{:S(2)}) copy-start(bf16[896,1024]{1,0:T(8,128)(2,1)} %param.19) | copy-start | bytes 5505028
  7.2 4.0 copy-start.2
  7.2 95.4 %all-reduce.8.cloned.1.call-start = ((), (), s32[]{:S(2)}) async-start(), calls=%async_computation.6 | async-start | bytes 5505024 | tf_op jit(solution)/shard_map/psum | solution.py:39
  7.2 4.0 copy-start.12
  13.3 0.9 copy-start.5
  16.5 86.1 %copy-start.13 = (f32[896]{0:T(1024)S(1)}, f32[896]{0:T(1024)}, u32[]{:S(2)}) copy-start(f32[896]{0:T(1024)} %param.18) | copy-start | bytes 10756
  16.5 86.1 %copy-start.14 = (f32[896]{0:T(1024)S(1)}, f32[896]{0:T(1024)}, u32[]{:S(2)}) copy-start(f32[896]{0:T(1024)} %param.17) | copy-start | bytes 10756
  16.5 225.9 %all-to-all-start = ((bf16[32,1,384,128]{2,3,1,0:T(8,128)(2,1)}), bf16[32,1,384,128]{2,3,1,0:T(8,128)(2,1)}, u32[]{:S(2)}, u32[]{:S(2)}) async-start(bf16[32,1,384,128]{2,3,1,0:T(8,128)(2,1)} %stack.2), calls=%async_computation | async-start | bytes 6291456 | tf_op jit(solution)/shard_map/all_to_all | solution.py:47
  25.3 198.2 %all-reduce.6.cloned.1.call-start = ((), (), s32[]{:S(2)}) async-start(), calls=%async_computation.3 | async-start | bytes 3145728 | tf_op jit(solution)/shard_map/psum | solution.py:42
  106.5 117.0 %copy-start.7 = (f32[1024]{0:T(1024)S(1)}, f32[1024]{0:T(1024)}, u32[]{:S(2)}) copy-start(f32[1024]{0:T(1024)} %param.20) | copy-start | bytes 12292
  106.5 132.7 %copy-start.8 = (f32[1024]{0:T(1024)S(1)}, f32[1024]{0:T(1024)}, u32[]{:S(2)}) copy-start(f32[1024]{0:T(1024)} %param.21) | copy-start | bytes 12292
  106.5 169.4 %reduce-scatter.7.cloned.1.call-start = ((), (), s32[]{:S(2)}) async-start(), calls=%async_computation.4 | async-start | bytes 884736
  223.5 15.8 %copy-start.1 = (f32[384,1024]{1,0:T(8,128)S(1)}, f32[384,1024]{1,0:T(8,128)}, u32[]{:S(2)}) copy-start(f32[384,1024]{1,0:T(8,128)} %all-reduce.6.cloned.1.call-done) | copy-start | bytes 4718596
  239.3 3.1 copy-start.9
  242.3 194.5 %reduce-scatter.9.cloned.1.call-start = ((), (), s32[]{:S(2)}) async-start(), calls=%async_computation.5 | async-start | bytes 884736
  242.4 2.7 copy-start.6
  245.1 3.1 copy-start.11
  345.7 62.8 %copy-start.3 = (f32[48,500]{0,1:T(8,128)}, f32[48,500]{0,1:T(8,128)S(1)}, u32[]{:S(2)}) copy-start(f32[48,500]{0,1:T(8,128)S(1)} %copy.32) | copy-start | bytes 288004
  408.6 29.2 %copy-start.4 = (f32[48,500]{0,1:T(8,128)S(1)}, f32[48,500]{0,1:T(8,128)}, u32[]{:S(2)}) copy-start(f32[48,500]{0,1:T(8,128)} %copy-done.3) | copy-start | bytes 288004
  408.6 159.6 %copy-start.10 = (s32[48]{0:T(128)S(1)}, s32[48]{0:T(128)}, u32[]{:S(2)}) copy-start(s32[48]{0:T(128)} %param.27) | copy-start | bytes 580
Sparse Core Ops, SparseCore 0:
  13.4 89.0 all-reduce.7
  106.7 116.7 all-reduce.5
  242.4 33.4 reduce-scatter.6
  409.9 26.8 reduce-scatter.8
